TPU v7x, 1024 devices: a whole 8x8x8 slice. The times are simulated.
1024 devices in a mesh: dp: 16 (over y, z_lo), mp: 64 (over x, z_hi, core).
Axes of the slice: x: 8, y: 8, z: 8 (z_hi: 4, z_lo: 2; z = z_hi * 2 + z_lo), core: 2. Of those that a mesh axis runs over, the one named last changes fastest.
Arguments:
- tokens: bfloat16 [4096, 4096], P('dp'), may hold values from -96 to 96
- inner_weight: float32 [2, 4096, 16384], P(None, 'dp', 'mp'), may hold values from -5 to 5, as said below
- inner_grad: float32 [2, 4096, 16384], P(None, 'dp', 'mp'), may hold values from -400 to 400
- inner_row: float32 [2, 4096], P(None, 'dp'), may hold values from 0.01 to 1
- inner_col: float32 [2, 16384], P(None, 'mp'), may hold values from 0.01 to 1
- outer_weight: float32 [16384, 4096], P('mp', 'dp'), may hold values from -5 to 5, as said below
- outer_grad: float32 [16384, 4096], P('mp', 'dp'), may hold values from -400 to 400
- outer_row: float32 [16384], P('mp'), may hold values from 0.01 to 1
- outer_col: float32 [4096], P('dp'), may hold values from 0.01 to 1
Outputs:
- inner_new: float32 [2, 4096, 16384], P(None, 'dp', 'mp')
- inner_update: float32 [2, 4096, 16384], P(None, 'dp', 'mp')
- inner_row_new: float32 [2, 4096], P(None, 'dp')
- inner_col_new: float32 [2, 16384], P(None, 'mp')
- outer_new: float32 [16384, 4096], P('mp', 'dp')
- outer_update: float32 [16384, 4096], P('mp', 'dp')
- outer_row_new: float32 [16384], P('mp')
- outer_col_new: float32 [4096], P('dp')
- hidden: bfloat16 [4096, 16384], P('dp', 'mp')
Inputs may be any that keep to these rules, and one draw needn't show every extreme that they name: `inner_weight`: parameters of the gate and up projections. `outer_weight`: parameters of the down projection.
All inputs are finite; a program needn't handle non-finite values.
Results may differ from a plain program's by a relative error of at most 0.0058.
Values may be sent and summed in bfloat16 or wider, within the bound.
A program may use at most 32 MiB of HBM per device.

v0:
```python
import jax
import jax.numpy as jnp
from jax import lax
from jax.sharding import PartitionSpec as P

D = 4096
FF = 16384
STEP = 10


def per_device(
    tokens,
    inner_weight,
    inner_grad,
    inner_row,
    inner_col,
    outer_weight,
    outer_grad,
    outer_row,
    outer_col,
):
    forget = 1.0 - STEP ** (-0.8)
    fresh = 1.0 - forget
    relative = min(0.01, STEP ** (-0.5))
    model_count = lax.axis_size("mp")
    data_count = lax.axis_size("dp")
    inner_square = inner_grad * inner_grad + 1e-30
    outer_square = outer_grad * outer_grad + 1e-30
    inner_param_sq = jnp.sum(inner_weight * inner_weight, axis=(1, 2))
    outer_param_sq = jnp.sum(outer_weight * outer_weight)
    inner_rowsum, outer_colsum = lax.psum(
        (jnp.sum(inner_square, axis=2), jnp.sum(outer_square, axis=0)), "mp"
    )
    inner_colsum, outer_rowsum = lax.psum(
        (jnp.sum(inner_square, axis=1), jnp.sum(outer_square, axis=1)), "dp"
    )
    inner_row_new = forget * inner_row + fresh * (inner_rowsum / FF)
    inner_col_new = forget * inner_col + fresh * (inner_colsum / D)
    outer_row_new = forget * outer_row + fresh * (outer_rowsum / D)
    outer_col_new = forget * outer_col + fresh * (outer_colsum / FF)
    inner_total, outer_total, inner_norm, outer_norm = lax.psum(
        (
            jnp.sum(inner_row_new, axis=1) / model_count,
            jnp.sum(outer_row_new) / data_count,
            inner_param_sq,
            outer_param_sq,
        ),
        ("dp", "mp"),
    )
    inner_mean = inner_total / D
    outer_mean = outer_total / FF
    inner_vhat = inner_row_new[:, :, None] * inner_col_new[:, None, :] / inner_mean[:, None, None]
    inner_raw = inner_grad / jnp.sqrt(inner_vhat)
    outer_vhat = outer_row_new[:, None] * outer_col_new[None, :] / outer_mean
    outer_raw = outer_grad / jnp.sqrt(outer_vhat)
    inner_usq, outer_usq = lax.psum(
        (jnp.sum(inner_raw * inner_raw, axis=(1, 2)), jnp.sum(outer_raw * outer_raw)), ("dp", "mp")
    )
    inner_clip = jnp.maximum(1.0, jnp.sqrt(inner_usq / (D * FF)))
    outer_clip = jnp.maximum(1.0, jnp.sqrt(outer_usq / (D * FF)))
    inner_step = relative * jnp.sqrt(inner_norm / (D * FF))
    outer_step = relative * jnp.sqrt(outer_norm / (D * FF))
    inner_update = -(inner_step / inner_clip)[:, None, None] * inner_raw
    outer_update = -(outer_step / outer_clip) * outer_raw
    inner_new = inner_weight + inner_update
    outer_new = outer_weight + outer_update
    inner_cast = inner_new.astype(jnp.bfloat16)
    shard_rows = lax.all_gather(inner_cast, "dp", axis=1, tiled=True)
    gate_part = jnp.dot(tokens, shard_rows[0], preferred_element_type=jnp.float32)
    up_part = jnp.dot(tokens, shard_rows[1], preferred_element_type=jnp.float32)
    hidden = (jax.nn.gelu(gate_part, approximate=True) * up_part).astype(jnp.bfloat16)
    return (
        inner_new,
        inner_update,
        inner_row_new,
        inner_col_new,
        outer_new,
        outer_update,
        outer_row_new,
        outer_col_new,
        hidden,
    )


def solution(mesh):
    placed = (
        P("dp", None),
        P(None, "dp", "mp"),
        P(None, "dp", "mp"),
        P(None, "dp"),
        P(None, "mp"),
        P("mp", "dp"),
        P("mp", "dp"),
        P("mp"),
        P("dp"),
    )
    return jax.shard_map(
        per_device,
        mesh=mesh,
        in_specs=placed,
        out_specs=(
            P(None, "dp", "mp"),
            P(None, "dp", "mp"),
            P(None, "dp"),
            P(None, "mp"),
            P("mp", "dp"),
            P("mp", "dp"),
            P("mp"),
            P("dp"),
            P("dp", "mp"),
        ),
        check_vma=False,
    )
```

profile of v0, /device:TPU:14, one launch (start us, length us, event | category | flops | bytes accessed | tf_op | source)
XLA Modules:
  0.0 538.9 jit_solution(5276052230780738372)
XLA Ops:
  7.2 0.0 copy-start
  7.2 0.0 copy-start.1
  7.2 0.0 copy-start.3
  7.2 0.0 all-gather.2.cloned.1.call-start
  7.3 1.4 fusion.6
  8.6 1.1 fusion.15
  9.7 134.6 %all-reduce.2 = (f32[2,256]{1,0:T(2,128)S(1)}, f32[256]{0:T(256)S(1)}) all-reduce(f32[2,256]{1,0:T(2,128)S(1)} %get-tuple-element.19, f32[256]{0:T(256)S(1)} %get-tuple-element.20), channel_id=1, replica_groups=mesh['dp'=16,'mp'=64] {'mp'}, use_global_device_ids=true, to_apply=%region_3.0 | all-reduce | flops 768 | bytes 6144 | tf_op jit(solution)/shard_map/psum | solution.py:31
  144.3 0.8 fusion.21
  145.1 36.8 %all-reduce.3 = (f32[256]{0:T(256)S(1)}, f32[2,256]{1,0:T(2,128)S(1)}) all-reduce(f32[256]{0:T(256)S(1)} %get-tuple-element.21, f32[2,256]{1,0:T(2,128)S(1)} %get-tuple-element.18), channel_id=1, replica_groups=mesh['dp'=16,'mp'=64] {'dp'}, use_global_device_ids=true, to_apply=%region_13.0 | all-reduce | flops 768 | bytes 6144 | tf_op jit(solution)/shard_map/psum | solution.py:34
  181.9 1.3 fusion.20
  183.8 126.7 %all-reduce.1 = (f32[2]{0:T(128)S(1)}, f32[]{:T(128)}) all-reduce(f32[2]{0:T(128)S(1)} %broadcast_multiply_fusion.3, f32[]{:T(128)S(6)} %div.67), channel_id=1, replica_groups=mesh['dp'=16,'mp'=64] {'dp','mp'}, use_global_device_ids=true, to_apply=%region_7.0 | all-reduce | flops 3 | bytes 24 | tf_op jit(solution)/shard_map/psum | solution.py:41
  311.2 0.7 multiply_add_fusion.4
  311.8 0.7 multiply_add_fusion.2
  312.5 1.8 multiply_reduce_fusion.2
  314.4 1.5 multiply_reduce_fusion
  315.9 112.1 %all-reduce = (f32[2]{0:T(128)S(1)}, f32[2]{0:T(128)S(1)}, f32[]{:T(128)}, f32[]{:T(128)}) all-reduce(f32[2]{0:T(128)S(1)} %get-tuple-element.41, f32[2]{0:T(128)S(1)} %get-tuple-element.42, f32[]{:T(128)} %get-tuple-element.44, f32[]{:T(128)} %get-tuple-element.43), channel_id=1, replica_groups=mesh['dp'=16,'mp'=64] {'dp','mp'}, use_global_device_ids=true, to_apply=%region_9.0 | all-reduce | flops 6 | bytes 48 | tf_op jit(solution)/shard_map/psum | solution.py:56
  428.0 0.0 copy-done.1
  428.0 0.0 copy-done.3
  428.0 1.2 fusion.18
  429.3 0.0 all-gather.2.cloned.1.call-update
  429.3 0.0 copy-done.5
  429.3 0.0 copy-done.4
  430.7 0.0 copy-done.6
  430.7 0.0 copy-done.7
  430.7 0.0 copy-done.2
  430.8 1.9 fusion.19
  432.6 95.1 %all-gather.2.cloned.1.call-done = bf16[2,4096,256]{2,1,0:T(8,128)(2,1)} async-done(((bf16[2,256,256]{2,1,0:T(8,128)(2,1)}), bf16[2,4096,256]{2,1,0:T(8,128)(2,1)}) %all-gather.2.cloned.1.call-update) | async-done | bytes 4194320 | tf_op jit(solution)/shard_map/all_gather | solution.py:68
  527.8 0.0 copy-done
  527.8 2.5 fusion.14
  530.3 0.3 copy-done.8
  530.6 0.8 fusion.5
  531.3 0.8 copy.18
  (9 shorter events, 0.0 us)
Async XLA Ops:
  7.2 520.6 %copy-start = (bf16[256,4096]{1,0:T(8,128)(2,1)S(1)}, bf16[256,4096]{1,0:T(8,128)(2,1)}, u32[]{:S(2)}) copy-start(bf16[256,4096]{1,0:T(8,128)(2,1)} %param.9) | copy-start | bytes 6291460
  7.2 420.8 %copy-start.1 = (f32[2,256,256]{2,1,0:T(8,128)S(1)}, f32[2,256,256]{2,1,0:T(8,128)}, u32[]{:S(2)}) copy-start(f32[2,256,256]{2,1,0:T(8,128)} %param.11) | copy-start | bytes 1572868
  7.2 420.8 %copy-start.3 = (f32[2,256,256]{2,1,0:T(8,128)S(1)}, f32[2,256,256]{2,1,0:T(8,128)}, u32[]{:S(2)}) copy-start(f32[2,256,256]{2,1,0:T(8,128)} %param.10) | copy-start | bytes 1572868
  7.2 520.5 %all-gather.2.cloned.1.call-start = ((), (), s32[]{:S(2)}) async-start(), calls=%async_computation | async-start | bytes 4456448 | tf_op jit(solution)/shard_map/all_gather | solution.py:68
  145.1 284.2 %copy-start.5 = (f32[2,256]{1,0:T(2,128)}, f32[2,256]{1,0:T(2,128)S(1)}, u32[]{:S(2)}) copy-start(f32[2,256]{1,0:T(2,128)S(1)} %get-tuple-element.40) | copy-start | bytes 6148
  183.2 247.6 %copy-start.6 = (f32[256]{0:T(256)}, f32[256]{0:T(256)S(1)}, u32[]{:S(2)}) copy-start(f32[256]{0:T(256)S(1)} %get-tuple-element.38) | copy-start | bytes 3076
  311.8 118.9 %copy-start.7 = (f32[256]{0:T(256)}, f32[256]{0:T(256)S(1)}, u32[]{:S(2)}) copy-start(f32[256]{0:T(256)S(1)} %multiply_add_fusion.4) | copy-start | bytes 3076
  312.5 116.8 %copy-start.4 = (f32[2,256]{1,0:T(2,128)}, f32[2,256]{1,0:T(2,128)S(1)}, u32[]{:S(2)}) copy-start(f32[2,256]{1,0:T(2,128)S(1)} %multiply_add_fusion.2) | copy-start | bytes 6148
  312.5 118.2 %copy-start.2 = (f32[256,256]{1,0:T(8,128)S(1)}, f32[256,256]{1,0:T(8,128)}, u32[]{:S(2)}) copy-start(f32[256,256]{1,0:T(8,128)} %param.15) | copy-start | bytes 786436
  527.8 2.8 copy-start.8
Sparse Core Ops, SparseCore 0:
  429.4 98.3 all-gather.1
where the time goes:
time: 540 us; the launch traced here: 539 us
  blocking collectives  410 us (76%)
  waiting for transfers between devices  95.1 us (18%)
  between operations  16.9 us (3%)
  other arithmetic  12.4 us (2%)
    psum x1, blocking collectives, per_device(): lax.psum((jnp.sum(inner_square, axis=2), jnp.sum(outer_square, axis=0)),...  135 us
    psum x1, blocking collectives, per_device(): lax.psum((jnp.sum(inner_row_new, axis=1) / model_count, jnp.sum(outer_row...  127 us
    psum x1, blocking collectives, per_device(): lax.psum((jnp.sum(inner_raw * inner_raw, axis=(1, 2)), jnp.sum(outer_raw...  112 us
    all_gather x1, waiting for transfers between devices, per_device(): shard_rows = lax.all_gather(inner_cast, 'dp', axis=1, tiled=True)  95.1 us
    psum x1, blocking collectives, per_device(): lax.psum((jnp.sum(inner_square, axis=1), jnp.sum(outer_square, axis=1)),...  36.8 us
  transfers between devices with their start and end apart: 1, of which 1 were waited for; matrix products, arithmetic and copies ran while one was open for 0% of the time, Pallas kernels for 0%

commit v1 on v0

v1 whole, which is shorter than its diff:
```python
import functools

import jax
import jax.numpy as jnp
from jax import lax
from jax.experimental import pallas as pl
from jax.experimental.pallas import tpu as pltpu
from jax.sharding import PartitionSpec as P

D = 4096
FF = 16384
STEP = 10
FORGET = 1.0 - STEP ** (-0.8)
FRESH = 1.0 - FORGET
RELATIVE = min(0.01, STEP ** (-0.5))

NY = 8
B = 256
H = 128
CHUNKS = 4
C64 = 64
MESH = pl.DeviceIdType.MESH


def rows_to_lanes(q):
    return jnp.sum((q[:, :H] + q[:, H:]).T, axis=0, keepdims=True)


def lanes_to_rows(v):
    return jnp.concatenate(
        [jnp.broadcast_to(v[:, :H], (H, H)).T, jnp.broadcast_to(v[:, H:], (H, H)).T], axis=0
    )


def kernel(
    tok, iw, ig, irow, icol, ow, og, orow, ocol,
    inew, iupd, irow_new, icol_new, onew, oupd, orow_new, ocol_new, hid,
    g_v, w_v, raw, new_v, upd_v, tokbuf, agbuf, acc, zbuf, hid_v,
    dp1, mx, mz, dp2, snd, scal,
    load_sem, tok_sem, out_sem, st_send, st_recv, tx_send, tx_recv, sib_send, sib_recv,
    ag_send, ag_recv, z_send, z_recv,
):
    dp, mp = lax.axis_index("dp"), lax.axis_index("mp")
    y, z = dp // 2, lax.rem(dp, 2)
    x, zc = mp // 8, lax.rem(mp, 8)
    core = lax.rem(mp, 2)

    def dp_peer(k):
        return (lax.rem(dp + k, 16), mp)

    def x_peer(k):
        return (dp, lax.rem(x + k, 8) * 8 + zc)

    def zc_peer(k):
        return (dp, x * 8 + lax.rem(zc + k, 8))

    y_next = (lax.rem(y + 1, NY) * 2 + z, mp)
    y_prev = (lax.rem(y + NY - 1, NY) * 2 + z, mp)
    z_pair = (y * 2 + 1 - z, mp)
    sibling = (dp, mp + 1 - 2 * core)

    barrier = pltpu.get_barrier_semaphore()
    for k in range(1, 16):
        pl.semaphore_signal(barrier, inc=1, device_id=dp_peer(k), device_id_type=MESH)
    for k in range(1, 8):
        pl.semaphore_signal(barrier, inc=1, device_id=x_peer(k), device_id_type=MESH)
        pl.semaphore_signal(barrier, inc=1, device_id=zc_peer(k), device_id_type=MESH)

    loads = [
        pltpu.make_async_copy(ig, g_v.at[pl.ds(0, 2)], load_sem.at[0]),
        pltpu.make_async_copy(og, g_v.at[2], load_sem.at[1]),
        pltpu.make_async_copy(iw, w_v.at[pl.ds(0, 2)], load_sem.at[2]),
        pltpu.make_async_copy(ow, w_v.at[2], load_sem.at[3]),
    ]
    for c in loads:
        c.start()
    own_tok = []
    for b in range(NY):
        c = pltpu.make_async_copy(
            tok.at[:, pl.ds(pl.multiple_of((2 * b + z) * B, B), B)],
            tokbuf.at[b, pl.ds(0, B), :],
            tok_sem.at[b],
        )
        c.start()
        own_tok.append(c)

    loads[0].wait()
    for k in range(2):
        g = g_v[k]
        v = jnp.sum(g * g + 1e-30, axis=0, keepdims=True)
        snd[0, 2 * k : 2 * k + 1, :] = v[:, :H]
        snd[0, 2 * k + 1 : 2 * k + 2, :] = v[:, H:]
    loads[1].wait()
    g = g_v[2]
    v = rows_to_lanes(g * g + 1e-30)
    snd[0, 4:5, :] = v[:, :H]
    snd[0, 5:6, :] = v[:, H:]
    snd[0, 6:8, :] = jnp.zeros((2, H), jnp.float32)

    pl.semaphore_wait(barrier, 29)

    def exchange(slot, me, peers, src, row0, stage):
        rows = slot.shape[1]
        for p in peers:
            pltpu.make_async_remote_copy(
                src_ref=src, dst_ref=slot.at[me], send_sem=st_send.at[stage], recv_sem=st_recv.at[stage],
                device_id=p, device_id_type=MESH,
            ).start()

    def arrived(slot, stage, n):
        part = slot.at[pl.ds(0, n)]
        pltpu.make_async_copy(part, part, st_recv.at[stage]).wait()

    def sent(slot, stage, n):
        part = slot.at[pl.ds(0, n)]
        pltpu.make_async_copy(part, part, st_send.at[stage]).wait()

    exchange(dp1, dp, [dp_peer(k) for k in range(1, 16)], snd.at[0, pl.ds(0, 8)], 0, 0)
    dp1[dp] = snd[0, 0:8, :]

    tok_out = []
    for j in range(4):
        b = core * 4 + j
        c = pltpu.make_async_remote_copy(
            src_ref=tok.at[:, pl.ds(pl.multiple_of((2 * b + 1 - z) * B, B), B)],
            dst_ref=tokbuf.at[b, pl.ds(B, B), :],
            send_sem=tx_send.at[j], recv_sem=tx_recv.at[j],
            device_id=z_pair, device_id_type=MESH,
        )
        c.start()
        tok_out.append(c)

    for k in range(2):
        g = g_v[k]
        v = rows_to_lanes(g * g + 1e-30)
        snd[1, 2 * k : 2 * k + 1, :] = v[:, :H]
        snd[1, 2 * k + 1 : 2 * k + 2, :] = v[:, H:]
    g = g_v[2]
    v = jnp.sum(g * g + 1e-30, axis=0, keepdims=True)
    snd[1, 4:5, :] = v[:, :H]
    snd[1, 5:6, :] = v[:, H:]
    loads[2].wait()
    loads[3].wait()
    for k in range(3):
        w = w_v[k]
        v = jnp.sum(w * w, axis=0, keepdims=True)
        snd[1, 12 + k : 13 + k, :] = v[:, :H] + v[:, H:]

    arrived(dp1, 0, 15)
    tot = dp1[0]
    for i in range(1, 16):
        tot = tot + dp1[i]
    scal[0:8, :] = tot

    old = [icol[0:1, :], icol[1:2, :], orow[...]]
    fc = []
    for k in range(3):
        s = jnp.concatenate([scal[2 * k : 2 * k + 1, :], scal[2 * k + 1 : 2 * k + 2, :]], axis=1)
        fc.append(FORGET * old[k] + FRESH * (s / D))
    icol_new[0:1, :] = fc[0]
    icol_new[1:2, :] = fc[1]
    orow_new[...] = fc[2]
    snd[1, 15:16, :] = fc[2][:, :H] + fc[2][:, H:]
    for k in range(2):
        g = g_v[k]
        v = rows_to_lanes(g * g * (1.0 / fc[k]))
        snd[1, 6 + 2 * k : 7 + 2 * k, :] = v[:, :H]
        snd[1, 7 + 2 * k : 8 + 2 * k, :] = v[:, H:]
    g = g_v[2]
    c2 = lanes_to_rows(lax.rsqrt(fc[2]))
    c2 = jnp.concatenate([c2, c2], axis=1)
    gs = g * c2
    v = jnp.sum(gs * gs, axis=0, keepdims=True)
    snd[1, 10:11, :] = v[:, :H]
    snd[1, 11:12, :] = v[:, H:]
    raw[2] = gs

    exchange(mx, x, [x_peer(k) for k in range(1, 8)], snd.at[1], 0, 1)
    mx[x] = snd[1]
    for k in range(2):
        raw[k] = g_v[k] * lax.rsqrt(fc[k])
    arrived(mx, 1, 7)
    tot = mx[0]
    for i in range(1, 8):
        tot = tot + mx[i]
    snd[2] = tot
    exchange(mz, zc, [zc_peer(k) for k in range(1, 8)], snd.at[2], 0, 2)
    mz[zc] = snd[2]
    sib_out = []
    for j in range(4):
        b = core * 4 + j
        tok_out[j].wait_recv()
        c = pltpu.make_async_remote_copy(
            src_ref=tokbuf.at[b, pl.ds(B, B), :],
            dst_ref=tokbuf.at[b, pl.ds(B, B), :],
            send_sem=sib_send.at[j], recv_sem=sib_recv.at[j],
            device_id=sibling, device_id_type=MESH,
        )
        c.start()
        sib_out.append(c)
    arrived(mz, 2, 7)
    tot = mz[0]
    for i in range(1, 8):
        tot = tot + mz[i]
    scal[16:32, :] = tot

    old = [irow[0:1, :], irow[1:2, :], ocol[...]]
    fr = []
    for k in range(3):
        r = 16 + 2 * k
        s = jnp.concatenate([scal[r : r + 1, :], scal[r + 1 : r + 2, :]], axis=1)
        f = FORGET * old[k] + FRESH * (s / FF)
        fr.append(f)
        r = 22 + 2 * k
        t = jnp.concatenate([scal[r : r + 1, :], scal[r + 1 : r + 2, :]], axis=1)
        u = t / f
        snd[3, k : k + 1, :] = u[:, :H] + u[:, H:]
        snd[3, 3 + k : 4 + k, :] = scal[28 + k : 29 + k, :]
    irow_new[0:1, :] = fr[0]
    irow_new[1:2, :] = fr[1]
    ocol_new[...] = fr[2]
    for k in range(2):
        snd[3, 6 + k : 7 + k, :] = fr[k][:, :H] + fr[k][:, H:]
    exchange(dp2, dp, [dp_peer(k) for k in range(1, 16)], snd.at[3, pl.ds(0, 8)], 0, 3)
    dp2[dp] = snd[3, 0:8, :]

    for k in range(2):
        rr = lanes_to_rows(lax.rsqrt(fr[k]))
        raw[k] = raw[k] * jnp.concatenate([rr, rr], axis=1)
    raw[2] = raw[2] * lax.rsqrt(fr[2])
    mean2 = jnp.sum(scal[31:32, :], axis=1, keepdims=True) / FF

    arrived(dp2, 3, 15)
    tot = dp2[0]
    for i in range(1, 16):
        tot = tot + dp2[i]
    scal[0:8, :] = jnp.broadcast_to(jnp.sum(tot, axis=1, keepdims=True), (8, H))

    coef = []
    for k in range(3):
        mean = scal[6 + k : 7 + k, 0:1] / D if k < 2 else mean2
        clip = jnp.maximum(1.0, jnp.sqrt(scal[k : k + 1, 0:1] * mean / (D * FF)))
        step = RELATIVE * jnp.sqrt(scal[3 + k : 4 + k, 0:1] / (D * FF))
        coef.append(step / clip * jnp.sqrt(mean))

    for k in range(2):
        u = raw[k] * (-coef[k])
        upd_v[k] = u
        new_v[k] = w_v[k] + u

    def ag_copy(way, c, s):
        src = lax.rem(y + NY - (s - 1), NY) if way == 0 else lax.rem(y + s - 1, NY)
        return pltpu.make_async_remote_copy(
            src_ref=agbuf.at[c, src], dst_ref=agbuf.at[c, src],
            send_sem=ag_send.at[way, c, s - 1], recv_sem=ag_recv.at[way, c, s - 1],
            device_id=y_next if way == 0 else y_prev, device_id_type=MESH,
        )

    def steps(way, c):
        return 4 if (c % 2 == 0) == (way == 0) else 3

    for c in range(CHUNKS):
        lo = c * C64
        block = jnp.concatenate([new_v[0, :, lo : lo + C64], new_v[1, :, lo : lo + C64]], axis=1)
        agbuf[c, y] = block.astype(jnp.bfloat16)
        for way in range(2):
            ag_copy(way, c, 1).start()

    u = raw[2] * (-coef[2])
    upd_v[2] = u
    new_v[2] = w_v[2] + u
    outs = [
        pltpu.make_async_copy(new_v.at[pl.ds(0, 2)], inew, out_sem.at[0]),
        pltpu.make_async_copy(upd_v.at[pl.ds(0, 2)], iupd, out_sem.at[1]),
        pltpu.make_async_copy(new_v.at[2], onew, out_sem.at[2]),
        pltpu.make_async_copy(upd_v.at[2], oupd, out_sem.at[3]),
    ]
    for c in outs:
        c.start()

    for c in own_tok:
        c.wait()
    for c in sib_out:
        c.wait()

    def product(c, b, first):
        part = jnp.dot(tokbuf[b], agbuf[c, b], preferred_element_type=jnp.float32)
        if first:
            acc[c] = part
        else:
            acc[c] += part

    for c in range(CHUNKS):
        product(c, y, True)

    z_out = [
        pltpu.make_async_remote_copy(
            src_ref=acc.at[c, pl.ds(B, B), :], dst_ref=zbuf.at[c],
            send_sem=z_send.at[c], recv_sem=z_recv.at[c],
            device_id=z_pair, device_id_type=MESH,
        )
        for c in range(CHUNKS)
    ]
    for s in range(1, 5):
        for c in range(CHUNKS):
            for way in range(2):
                if s > steps(way, c):
                    continue
                ag_copy(way, c, s).wait_recv()
                if s < steps(way, c):
                    ag_copy(way, c, s + 1).start()
                b = lax.rem(y + NY - s, NY) if way == 0 else lax.rem(y + s, NY)
                product(c, b, False)
            if s == 4:
                z_out[c].start()

    lane = lax.broadcasted_iota(jnp.int32, (B, H), 1)
    hid_out = []
    for p in range(CHUNKS // 2):
        both = []
        for c in (2 * p, 2 * p + 1):
            z_out[c].wait_recv()
            both.append(acc[c, 0:B, :] + zbuf[c])
        left, right = both
        gate = jnp.where(lane < C64, left, pltpu.roll(right, C64, 1))
        up = jnp.where(lane < C64, pltpu.roll(left, C64, 1), right)
        hid_v[p] = (jax.nn.gelu(gate, approximate=True) * up).astype(jnp.bfloat16)
        c = pltpu.make_async_copy(hid_v.at[p], hid.at[:, pl.ds(p * H, H)], out_sem.at[4 + p])
        c.start()
        hid_out.append(c)

    sent(dp1, 0, 15)
    sent(mx, 1, 7)
    sent(mz, 2, 7)
    sent(dp2, 3, 15)
    for c in tok_out:
        c.wait_send()
    for c in range(CHUNKS):
        for way in range(2):
            for s in range(1, steps(way, c) + 1):
                ag_copy(way, c, s).wait_send()
        z_out[c].wait_send()
    for c in outs:
        c.wait()
    for c in hid_out:
        c.wait()


def per_device(tokens, iw, ig, irow, icol, ow, og, orow, ocol):
    f32, bf16 = jnp.float32, jnp.bfloat16
    hbm = pl.BlockSpec(memory_space=pl.ANY)
    vm = pl.BlockSpec(memory_space=pltpu.VMEM)
    sds = jax.ShapeDtypeStruct
    outs = pl.pallas_call(
        kernel,
        out_shape=(
            sds((2, B, B), f32), sds((2, B, B), f32), sds((2, B), f32), sds((2, B), f32),
            sds((B, B), f32), sds((B, B), f32), sds((1, B), f32), sds((1, B), f32), sds((B, B), bf16),
        ),
        in_specs=[hbm, hbm, hbm, vm, vm, hbm, hbm, vm, vm],
        out_specs=(hbm, hbm, vm, vm, hbm, hbm, vm, vm, hbm),
        scratch_shapes=[
            pltpu.VMEM((3, B, B), f32),
            pltpu.VMEM((3, B, B), f32),
            pltpu.VMEM((3, B, B), f32),
            pltpu.VMEM((3, B, B), f32),
            pltpu.VMEM((3, B, B), f32),
            pltpu.VMEM((NY, 2 * B, B), bf16),
            pltpu.VMEM((CHUNKS, NY, B, H), bf16),
            pltpu.VMEM((CHUNKS, 2 * B, H), f32),
            pltpu.VMEM((CHUNKS, B, H), f32),
            pltpu.VMEM((CHUNKS // 2, B, H), bf16),
            pltpu.VMEM((16, 8, H), f32),
            pltpu.VMEM((8, 16, H), f32),
            pltpu.VMEM((8, 16, H), f32),
            pltpu.VMEM((16, 8, H), f32),
            pltpu.VMEM((4, 16, H), f32),
            pltpu.VMEM((32, H), f32),
            pltpu.SemaphoreType.DMA((4,)),
            pltpu.SemaphoreType.DMA((NY,)),
            pltpu.SemaphoreType.DMA((6,)),
            pltpu.SemaphoreType.DMA((4,)),
            pltpu.SemaphoreType.DMA((4,)),
            pltpu.SemaphoreType.DMA((4,)),
            pltpu.SemaphoreType.DMA((4,)),
            pltpu.SemaphoreType.DMA((4,)),
            pltpu.SemaphoreType.DMA((4,)),
            pltpu.SemaphoreType.DMA((2, CHUNKS, 4)),
            pltpu.SemaphoreType.DMA((2, CHUNKS, 4)),
            pltpu.SemaphoreType.DMA((CHUNKS,)),
            pltpu.SemaphoreType.DMA((CHUNKS,)),
        ],
        compiler_params=pltpu.CompilerParams(
            collective_id=0, has_side_effects=True, vmem_limit_bytes=40 * 1024 * 1024
        ),
        cost_estimate=pl.CostEstimate(
            flops=2 * B * D * 2 * B, bytes_accessed=5 * 1024 * 1024, transcendentals=B * B
        ),
    )(tokens, iw, ig, irow, icol, ow, og, orow.reshape(1, B), ocol.reshape(1, B))
    outs = list(outs)
    outs[6] = outs[6].reshape(B)
    outs[7] = outs[7].reshape(B)
    return tuple(outs)


def solution(mesh):
    placed = (
        P("dp", None),
        P(None, "dp", "mp"),
        P(None, "dp", "mp"),
        P(None, "dp"),
        P(None, "mp"),
        P("mp", "dp"),
        P("mp", "dp"),
        P("mp"),
        P("dp"),
    )
    return jax.shard_map(
        per_device,
        mesh=mesh,
        in_specs=placed,
        out_specs=(
            P(None, "dp", "mp"),
            P(None, "dp", "mp"),
            P(None, "dp"),
            P(None, "mp"),
            P("mp", "dp"),
            P("mp", "dp"),
            P("mp"),
            P("dp"),
            P("dp", "mp"),
        ),
        check_vma=False,
    )
```

time: 540 us -> 92.7 us (0.17)
  the two profiles are of different devices: /device:TPU:14 before, /device:TPU:16 now
where the time goes in v1:
time: 92.7 us; the launch traced here: 92.3 us
  Pallas kernels  77.4 us (83%)
  local copies, waits for them, and re-layouts  14.2 us (15%)
    pallas_call x1, Pallas kernels, per_device(): pl.pallas_call(kernel, out_shape=(sds((2, B, B), f32), sds((2, B, B), f32...  77.4 us
    unnamed x27, local copies, waits for them, and re-layouts  14.2 us

profile of v1, /device:TPU:16, one launch (start us, length us, event | category | flops | bytes accessed | tf_op | source)
XLA Modules:
  0.0 92.3 jit_solution(14700498500109525868)
XLA Ops:
  0.6 0.0 copy-start
  0.7 1.6 %copy-done = bf16[256,4096]{1,0:T(8,128)(2,1)S(1)} copy-done((bf16[256,4096]{1,0:T(8,128)(2,1)S(1)}, bf16[256,4096]{1,0:T(8,128)(2,1)}, u32[]{:S(2)}) %copy-start) | copy-done | bytes 2097176
  2.2 0.0 copy-start.1
  2.2 1.0 %copy-done.1 = f32[2,256,256]{2,1,0:T(8,128)S(1)} copy-done((f32[2,256,256]{2,1,0:T(8,128)S(1)}, f32[2,256,256]{2,1,0:T(8,128)}, u32[]{:S(2)}) %copy-start.1) | copy-done | bytes 524312
  3.3 0.0 copy-start.2
  3.3 1.0 %copy-done.2 = f32[2,256,256]{2,1,0:T(8,128)S(1)} copy-done((f32[2,256,256]{2,1,0:T(8,128)S(1)}, f32[2,256,256]{2,1,0:T(8,128)}, u32[]{:S(2)}) %copy-start.2) | copy-done | bytes 524312
  4.3 0.0 copy-start.3
  4.3 0.9 %copy-done.3 = f32[256,256]{1,0:T(8,128)S(1)} copy-done((f32[256,256]{1,0:T(8,128)S(1)}, f32[256,256]{1,0:T(8,128)}, u32[]{:S(2)}) %copy-start.3) | copy-done | bytes 262168
  5.3 0.0 copy-start.4
  5.3 0.9 %copy-done.4 = f32[256,256]{1,0:T(8,128)S(1)} copy-done((f32[256,256]{1,0:T(8,128)S(1)}, f32[256,256]{1,0:T(8,128)}, u32[]{:S(2)}) %copy-start.4) | copy-done | bytes 262168
  6.2 0.0 copy-start.5
  6.2 0.7 copy-done.5
  6.9 0.0 copy-start.6
  6.9 0.7 copy-done.6
  7.6 0.0 copy-start.7
  7.6 0.7 copy-done.7
  8.3 0.0 copy-start.8
  8.3 0.7 copy-done.8
  8.9 77.4 %shard_map.160 = (f32[2,256,256]{2,1,0:T(8,128)S(1)}, f32[2,256,256]{2,1,0:T(8,128)S(1)}, f32[2,256]{1,0:T(2,128)S(1)}, f32[2,256]{1,0:T(2,128)S(1)}, f32[256,25...) custom-call(bf16[256,4096]{1,0:T(8,128)(2,1)S(1)} %copy-done, ...), custom_call_target="tpu_custom_call" | custom-call | flops 1073741824 | bytes 5242880 | tf_op jit(solution)/shard_map/pallas_call | solution.py:354
  86.4 0.8 copy.27
  87.2 0.8 copy.28
  88.0 0.6 copy.29
  88.5 0.6 copy.30
  89.1 0.7 copy.31
  89.8 0.7 copy.32
  90.5 0.6 copy.33
  91.1 0.6 copy.34
  91.6 0.7 copy.35
Async XLA Ops:
  0.6 1.6 %copy-start = (bf16[256,4096]{1,0:T(8,128)(2,1)S(1)}, bf16[256,4096]{1,0:T(8,128)(2,1)}, u32[]{:S(2)}) copy-start(bf16[256,4096]{1,0:T(8,128)(2,1)} %tok.1) | copy-start | bytes 6291460
  2.2 1.0 %copy-start.1 = (f32[2,256,256]{2,1,0:T(8,128)S(1)}, f32[2,256,256]{2,1,0:T(8,128)}, u32[]{:S(2)}) copy-start(f32[2,256,256]{2,1,0:T(8,128)} %iw.1) | copy-start | bytes 1572868
  3.3 1.0 %copy-start.2 = (f32[2,256,256]{2,1,0:T(8,128)S(1)}, f32[2,256,256]{2,1,0:T(8,128)}, u32[]{:S(2)}) copy-start(f32[2,256,256]{2,1,0:T(8,128)} %ig.1) | copy-start | bytes 1572868
  4.3 0.9 %copy-start.3 = (f32[256,256]{1,0:T(8,128)S(1)}, f32[256,256]{1,0:T(8,128)}, u32[]{:S(2)}) copy-start(f32[256,256]{1,0:T(8,128)} %ow.1) | copy-start | bytes 786436
  5.3 0.9 %copy-start.4 = (f32[256,256]{1,0:T(8,128)S(1)}, f32[256,256]{1,0:T(8,128)}, u32[]{:S(2)}) copy-start(f32[256,256]{1,0:T(8,128)} %og.1) | copy-start | bytes 786436
  6.2 0.7 copy-start.5
  6.9 0.7 copy-start.6
  7.6 0.7 copy-start.7
  8.3 0.7 copy-start.8

commit v2 on v1

v2 whole, which is shorter than its diff:
```python
import functools

import jax
import jax.numpy as jnp
from jax import lax
from jax.experimental import pallas as pl
from jax.experimental.pallas import tpu as pltpu
from jax.sharding import PartitionSpec as P

D = 4096
FF = 16384
STEP = 10
FORGET = 1.0 - STEP ** (-0.8)
FRESH = 1.0 - FORGET
RELATIVE = min(0.01, STEP ** (-0.5))

NY = 8
B = 256
H = 128
CHUNKS = 4
EARLY = 2
STREAMS = 2 * EARLY + CHUNKS - EARLY
C64 = 64
MESH = pl.DeviceIdType.MESH


def rows_to_lanes(q):
    return jnp.sum((q[:, :H] + q[:, H:]).T, axis=0, keepdims=True)


def lanes_to_rows(v):
    return jnp.concatenate(
        [jnp.broadcast_to(v[:, :H], (H, H)).T, jnp.broadcast_to(v[:, H:], (H, H)).T], axis=0
    )


def far_first(n):
    return sorted(range(1, n), key=lambda k: -min(k, n - k))


def kernel(
    tok, iw, ig, irow, icol, ow, og, orow, ocol,
    inew, iupd, irow_new, icol_new, onew, oupd, orow_new, ocol_new, hid,
    g_v, w_v, raw, new_v, upd_v, tokbuf, agbuf, acc, zbuf, zout_v, zin_v, hid_v,
    dp1, rx, rz, tx, tz, dp2, snd, scal, rmat,
    load_sem, tok_sem, out_sem, st_send, st_recv, tx_send, tx_recv, sib_send, sib_recv,
    ag_send, ag_recv, z_send, z_recv,
):
    dp, mp = lax.axis_index("dp"), lax.axis_index("mp")
    y, z = dp // 2, lax.rem(dp, 2)
    x, zc = mp // 8, lax.rem(mp, 8)
    core = lax.rem(mp, 2)

    dp_peers = [(lax.rem(dp + k, 16), mp) for k in far_first(16)]
    x_peers = [(dp, lax.rem(x + k, 8) * 8 + zc) for k in far_first(8)]
    zc_peers = [(dp, x * 8 + lax.rem(zc + k, 8)) for k in far_first(8)]
    y_next = (lax.rem(y + 1, NY) * 2 + z, mp)
    y_prev = (lax.rem(y + NY - 1, NY) * 2 + z, mp)
    z_pair = (y * 2 + 1 - z, mp)
    sibling = (dp, mp + 1 - 2 * core)

    barrier = pltpu.get_barrier_semaphore()
    for peer in dp_peers + x_peers + zc_peers:
        pl.semaphore_signal(barrier, inc=1, device_id=peer, device_id_type=MESH)

    loads = [
        pltpu.make_async_copy(ig, g_v.at[pl.ds(0, 2)], load_sem.at[0]),
        pltpu.make_async_copy(og, g_v.at[2], load_sem.at[1]),
        pltpu.make_async_copy(iw, w_v.at[pl.ds(0, 2)], load_sem.at[2]),
        pltpu.make_async_copy(ow, w_v.at[2], load_sem.at[3]),
    ]
    for c in loads:
        c.start()
    own_tok = []
    for b in range(NY):
        c = pltpu.make_async_copy(
            tok.at[:, pl.ds(pl.multiple_of((2 * b + z) * B, B), B)],
            tokbuf.at[b, pl.ds(0, B), :],
            tok_sem.at[b],
        )
        c.start()
        own_tok.append(c)

    def put(i, row, v):
        snd[i, row : row + 1, :] = v[:, :H]
        snd[i, row + 1 : row + 2, :] = v[:, H:]

    def take(row):
        return jnp.concatenate([scal[row : row + 1, :], scal[row + 1 : row + 2, :]], axis=1)

    def exchange(slot, me, peers, src, stage):
        for p in peers:
            pltpu.make_async_remote_copy(
                src_ref=src, dst_ref=slot.at[me], send_sem=st_send.at[stage], recv_sem=st_recv.at[stage],
                device_id=p, device_id_type=MESH,
            ).start()
        slot[me] = src[...]

    def arrived(slot, stage):
        n = slot.shape[0]
        part = slot.at[pl.ds(0, n - 1)]
        pltpu.make_async_copy(part, part, st_recv.at[stage]).wait()
        tot = slot[0]
        for i in range(1, n):
            tot = tot + slot[i]
        return tot

    def sent(slot, stage):
        part = slot.at[pl.ds(0, slot.shape[0] - 1)]
        pltpu.make_async_copy(part, part, st_send.at[stage]).wait()

    def ag_copy(way, st, s):
        src = lax.rem(y + NY - (s - 1), NY) if way == 0 else lax.rem(y + s - 1, NY)
        return pltpu.make_async_remote_copy(
            src_ref=agbuf.at[st, src], dst_ref=agbuf.at[st, src],
            send_sem=ag_send.at[way, st, s - 1], recv_sem=ag_recv.at[way, st, s - 1],
            device_id=y_next if way == 0 else y_prev, device_id_type=MESH,
        )

    def steps(way, st):
        return 4 if (st % 2 == 0) == (way == 0) else 3

    def origin(way, s):
        return lax.rem(y + NY - s, NY) if way == 0 else lax.rem(y + s, NY)

    def launch(st, pair, c):
        lo = c * C64
        block = jnp.concatenate([pair[0, :, lo : lo + C64], pair[1, :, lo : lo + C64]], axis=1)
        agbuf[st, y] = block.astype(jnp.bfloat16)
        for way in range(2):
            ag_copy(way, st, 1).start()

    def relay(st, s):
        for way in range(2):
            if s <= steps(way, st):
                ag_copy(way, st, s).wait_recv()
                if s < steps(way, st):
                    ag_copy(way, st, s + 1).start()

    def product(st, b, first=False):
        part = jnp.dot(tokbuf[b], agbuf[st, b], preferred_element_type=jnp.float32)
        if first:
            acc[st] = part
        else:
            acc[st] += part

    def products(st, s):
        for way in range(2):
            if s <= steps(way, st):
                product(st, origin(way, s))

    snd[...] = jnp.zeros_like(snd)
    loads[0].wait()
    for k in range(2):
        g = g_v[k]
        put(0, 2 * k, jnp.sum(g * g + 1e-30, axis=0, keepdims=True))
    loads[1].wait()
    g = g_v[2]
    put(0, 4, rows_to_lanes(g * g + 1e-30))

    pl.semaphore_wait(barrier, 29)
    exchange(dp1, dp, dp_peers, snd.at[0], 0)

    loads[2].wait()
    for c in range(EARLY):
        launch(c, w_v, c)
    for c in range(EARLY):
        launch(EARLY + c, g_v, c)

    tok_out = []
    for j in range(4):
        b = core * 4 + j
        c = pltpu.make_async_remote_copy(
            src_ref=tok.at[:, pl.ds(pl.multiple_of((2 * b + 1 - z) * B, B), B)],
            dst_ref=tokbuf.at[b, pl.ds(B, B), :],
            send_sem=tx_send.at[j], recv_sem=tx_recv.at[j],
            device_id=z_pair, device_id_type=MESH,
        )
        c.start()
        tok_out.append(c)

    for k in range(2):
        g = g_v[k]
        put(1, 2 * k, rows_to_lanes(g * g + 1e-30))
    g = g_v[2]
    put(1, 4, jnp.sum(g * g + 1e-30, axis=0, keepdims=True))
    exchange(rx, x, x_peers, snd.at[1], 1)
    loads[3].wait()
    lane1 = lax.broadcasted_iota(jnp.int32, (1, H), 1)
    misc = jnp.zeros((1, H), jnp.float32)
    for k in range(3):
        w = w_v[k]
        v = jnp.sum(w * w, axis=0, keepdims=True)
        misc = jnp.where(lane1 == k, jnp.sum(v, axis=1, keepdims=True), misc)

    scal[0:8, :] = arrived(dp1, 0)
    old = [icol[0:1, :], icol[1:2, :], orow[...]]
    fc = [FORGET * old[k] + FRESH * (take(2 * k) / D) for k in range(3)]
    cc = [lax.rsqrt(f) for f in fc]
    misc = jnp.where(lane1 == 3, jnp.sum(fc[2], axis=1, keepdims=True), misc)
    snd[2, 6:7, :] = misc
    for k in range(2):
        g = g_v[k] * cc[k]
        raw[k] = g
        put(2, 2 * k, rows_to_lanes(g * g))
    c2 = lanes_to_rows(cc[2])
    g = g_v[2] * jnp.concatenate([c2, c2], axis=1)
    raw[2] = g
    put(2, 4, jnp.sum(g * g, axis=0, keepdims=True))
    exchange(tx, x, x_peers, snd.at[2], 2)
    icol_new[0:1, :] = fc[0]
    icol_new[1:2, :] = fc[1]
    orow_new[...] = fc[2]

    snd[3] = arrived(rx, 1)
    exchange(rz, zc, zc_peers, snd.at[3], 3)
    for st in range(2 * EARLY):
        relay(st, 1)
    snd[4] = arrived(tx, 2)
    exchange(tz, zc, zc_peers, snd.at[4], 4)

    sib_out = []
    for j in range(4):
        b = core * 4 + j
        tok_out[j].wait_recv()
        c = pltpu.make_async_remote_copy(
            src_ref=tokbuf.at[b, pl.ds(B, B), :],
            dst_ref=tokbuf.at[b, pl.ds(B, B), :],
            send_sem=sib_send.at[j], recv_sem=sib_recv.at[j],
            device_id=sibling, device_id_type=MESH,
        )
        c.start()
        sib_out.append(c)
    for st in range(2 * EARLY):
        relay(st, 2)

    scal[8:16, :] = arrived(rz, 3)
    scal[16:24, :] = arrived(tz, 4)
    old = [irow[0:1, :], irow[1:2, :], ocol[...]]
    fr = []
    for k in range(3):
        f = FORGET * old[k] + FRESH * (take(8 + 2 * k) / FF)
        fr.append(f)
        u = take(16 + 2 * k) / f
        snd[5, k : k + 1, :] = u[:, :H] + u[:, H:]
    snd[5, 3:4, :] = scal[22:23, :]
    put(5, 4, fr[0])
    put(5, 6, fr[1])
    exchange(dp2, dp, dp_peers, snd.at[5], 5)
    irow_new[0:1, :] = fr[0]
    irow_new[1:2, :] = fr[1]
    ocol_new[...] = fr[2]
    mean2 = scal[22:23, 3:4] / FF

    for k in range(2):
        rr = lanes_to_rows(lax.rsqrt(fr[k]))
        raw[k] = raw[k] * jnp.concatenate([rr, rr], axis=1)
    raw[2] = raw[2] * lax.rsqrt(fr[2])

    for c in own_tok:
        c.wait()
    for c in sib_out:
        c.wait()
    for st in range(EARLY):
        product(st, y, True)
    for st in range(EARLY):
        products(st, 1)
    for st in range(2 * EARLY):
        relay(st, 3)
    for st in range(EARLY):
        products(st, 2)

    scal[0:8, :] = arrived(dp2, 5)
    s = [jnp.sum(scal[k : k + 1, :], axis=1, keepdims=True) for k in range(3)]
    mean = [jnp.sum(take(4 + 2 * k), axis=1, keepdims=True) / D for k in range(2)] + [mean2]
    coef = []
    for k in range(3):
        clip = jnp.maximum(1.0, jnp.sqrt(s[k] * mean[k] / (D * FF)))
        step = RELATIVE * jnp.sqrt(scal[3:4, k : k + 1] / (D * FF))
        coef.append(step / clip * jnp.sqrt(mean[k]))

    for k in range(2):
        u = raw[k] * (-coef[k])
        upd_v[k] = u
        new_v[k] = w_v[k] + u
    for c in range(EARLY, CHUNKS):
        launch(EARLY + c, new_v, c)

    for st in range(EARLY):
        products(st, 3)
    z_copies = []
    for st in range(EARLY):
        relay(st, 4)
        products(st, 4)
        c = pltpu.make_async_remote_copy(
            src_ref=acc.at[st, pl.ds(B, B), :], dst_ref=zbuf.at[st],
            send_sem=z_send.at[st], recv_sem=z_recv.at[st], device_id=z_pair, device_id_type=MESH,
        )
        c.start()
        z_copies.append(c)

    def z_exchange(st):
        i = st - EARLY
        zout_v[i] = acc[st, B : 2 * B, :].astype(jnp.bfloat16)
        c = pltpu.make_async_remote_copy(
            src_ref=zout_v.at[i], dst_ref=zin_v.at[i],
            send_sem=z_send.at[st], recv_sem=z_recv.at[st], device_id=z_pair, device_id_type=MESH,
        )
        c.start()
        z_copies.append(c)

    u = raw[2] * (-coef[2])
    upd_v[2] = u
    new_v[2] = w_v[2] + u
    outs = [
        pltpu.make_async_copy(new_v.at[pl.ds(0, 2)], inew, out_sem.at[0]),
        pltpu.make_async_copy(upd_v.at[pl.ds(0, 2)], iupd, out_sem.at[1]),
        pltpu.make_async_copy(new_v.at[2], onew, out_sem.at[2]),
        pltpu.make_async_copy(upd_v.at[2], oupd, out_sem.at[3]),
    ]
    for c in outs:
        c.start()

    late = range(2 * EARLY, STREAMS)
    for st in late:
        relay(st, 1)

    rmat[...] = jnp.ones((H, H), jnp.float32)
    for b in range(NY):
        rmat[4 * b : 4 * b + 4, :] = lax.rsqrt(dp2[2 * b + z, 4:8, :])
    rmat[...] = rmat[...].T
    for st in range(EARLY, 2 * EARLY):
        relay(st, 4)
    low = lax.broadcasted_iota(jnp.int32, (H, H), 1) < C64

    def scaled_products(b):
        halves = []
        for h in range(2):
            j = 4 * b + h
            halves.append(
                jnp.where(
                    low,
                    jnp.broadcast_to(rmat[:, j : j + 1], (H, H)),
                    jnp.broadcast_to(rmat[:, j + 2 : j + 3], (H, H)),
                )
            )
        rr = jnp.concatenate(halves, axis=0)
        for st in range(EARLY, 2 * EARLY):
            rows = (agbuf[st, b].astype(jnp.float32) * rr).astype(jnp.bfloat16)
            part = jnp.dot(tokbuf[b], rows, preferred_element_type=jnp.float32)
            if b == 0:
                acc[st] = part
            else:
                acc[st] += part

    for b in range(0, 4):
        scaled_products(b)
    for st in late:
        product(st, y, True)
    for st in late:
        relay(st, 2)
    for b in range(4, NY):
        scaled_products(b)
    for st in range(EARLY, 2 * EARLY):
        z_exchange(st)
    for st in late:
        products(st, 1)
    for st in late:
        relay(st, 3)
    for st in late:
        products(st, 2)
    for st in late:
        products(st, 3)
    for st in late:
        relay(st, 4)
        products(st, 4)
        z_exchange(st)

    lane = lax.broadcasted_iota(jnp.int32, (B, H), 1)
    hid_out = []

    def finish(p, left, right):
        gate = jnp.where(lane < C64, left, pltpu.roll(right, C64, 1))
        up = jnp.where(lane < C64, pltpu.roll(left, C64, 1), right)
        hid_v[p] = (jax.nn.gelu(gate, approximate=True) * up).astype(jnp.bfloat16)
        c = pltpu.make_async_copy(hid_v.at[p], hid.at[:, pl.ds(p * H, H)], out_sem.at[4 + p])
        c.start()
        hid_out.append(c)

    both = []
    for st in range(EARLY):
        lo = st * C64
        z_copies[st].wait_recv()
        z_copies[EARLY + st].wait_recv()
        scale = jnp.concatenate([cc[k][:, lo : lo + C64] * coef[k] for k in range(2)], axis=1)
        step_part = acc[EARLY + st, 0:B, :] + zin_v[st].astype(jnp.float32)
        both.append(acc[st, 0:B, :] + zbuf[st] - step_part * scale)
    finish(0, both[0], both[1])
    both = []
    for st in late:
        z_copies[st].wait_recv()
        both.append(acc[st, 0:B, :] + zin_v[st - EARLY].astype(jnp.float32))
    finish(1, both[0], both[1])

    for stage, slot in enumerate((dp1, rx, tx, rz, tz, dp2)):
        sent(slot, stage)
    for c in tok_out + z_copies:
        c.wait_send()
    for st in range(STREAMS):
        for way in range(2):
            for t in range(1, steps(way, st) + 1):
                ag_copy(way, st, t).wait_send()
    for c in outs + hid_out:
        c.wait()


def copy_kernel(*refs):
    sems = refs[-1]
    n = (len(refs) - 1) // 2
    copies = [pltpu.make_async_copy(refs[i], refs[n + i], sems.at[i]) for i in range(n)]
    for c in copies:
        c.start()
    for c in copies:
        c.wait()


def per_device(tokens, iw, ig, irow, icol, ow, og, orow, ocol):
    f32, bf16 = jnp.float32, jnp.bfloat16
    hbm = pl.BlockSpec(memory_space=pl.ANY)
    vm = pl.BlockSpec(memory_space=pltpu.VMEM)
    sds = jax.ShapeDtypeStruct
    shapes = (
        sds((2, B, B), f32), sds((2, B, B), f32), sds((2, B), f32), sds((2, B), f32),
        sds((B, B), f32), sds((B, B), f32), sds((1, B), f32), sds((1, B), f32), sds((B, B), bf16),
    )
    dma = pltpu.SemaphoreType.DMA
    outs = pl.pallas_call(
        kernel,
        out_shape=shapes,
        in_specs=[hbm, hbm, hbm, vm, vm, hbm, hbm, vm, vm],
        out_specs=(hbm, hbm, vm, vm, hbm, hbm, vm, vm, hbm),
        scratch_shapes=[
            pltpu.VMEM((3, B, B), f32),
            pltpu.VMEM((3, B, B), f32),
            pltpu.VMEM((3, B, B), f32),
            pltpu.VMEM((3, B, B), f32),
            pltpu.VMEM((3, B, B), f32),
            pltpu.VMEM((NY, 2 * B, B), bf16),
            pltpu.VMEM((STREAMS, NY, B, H), bf16),
            pltpu.VMEM((STREAMS, 2 * B, H), f32),
            pltpu.VMEM((EARLY, B, H), f32),
            pltpu.VMEM((CHUNKS, B, H), bf16),
            pltpu.VMEM((CHUNKS, B, H), bf16),
            pltpu.VMEM((CHUNKS // 2, B, H), bf16),
            pltpu.VMEM((16, 8, H), f32),
            pltpu.VMEM((8, 8, H), f32),
            pltpu.VMEM((8, 8, H), f32),
            pltpu.VMEM((8, 8, H), f32),
            pltpu.VMEM((8, 8, H), f32),
            pltpu.VMEM((16, 8, H), f32),
            pltpu.VMEM((6, 8, H), f32),
            pltpu.VMEM((24, H), f32),
            pltpu.VMEM((H, H), f32),
            dma((4,)), dma((NY,)), dma((6,)), dma((6,)), dma((6,)), dma((4,)), dma((4,)), dma((4,)), dma((4,)),
            dma((2, STREAMS, 4)), dma((2, STREAMS, 4)), dma((STREAMS,)), dma((STREAMS,)),
        ],
        compiler_params=pltpu.CompilerParams(
            collective_id=0, has_side_effects=True, vmem_limit_bytes=63 * 1024 * 1024
        ),
        cost_estimate=pl.CostEstimate(
            flops=2 * B * D * 2 * B, bytes_accessed=5 * 1024 * 1024, transcendentals=B * B
        ),
    )(tokens, iw, ig, irow, icol, ow, og, orow.reshape(1, B), ocol.reshape(1, B))
    outs = pl.pallas_call(
        copy_kernel,
        out_shape=shapes,
        in_specs=[hbm] * len(shapes),
        out_specs=(hbm,) * len(shapes),
        scratch_shapes=[dma((len(shapes),))],
    )(*outs)
    outs = list(outs)
    outs[6] = outs[6].reshape(B)
    outs[7] = outs[7].reshape(B)
    return tuple(outs)


def solution(mesh):
    placed = (
        P("dp", None),
        P(None, "dp", "mp"),
        P(None, "dp", "mp"),
        P(None, "dp"),
        P(None, "mp"),
        P("mp", "dp"),
        P("mp", "dp"),
        P("mp"),
        P("dp"),
    )
    return jax.shard_map(
        per_device,
        mesh=mesh,
        in_specs=placed,
        out_specs=(
            P(None, "dp", "mp"),
            P(None, "dp", "mp"),
            P(None, "dp"),
            P(None, "mp"),
            P("mp", "dp"),
            P("mp", "dp"),
            P("mp"),
            P("dp"),
            P("dp", "mp"),
        ),
        check_vma=False,
    )
```

time: 92.7 us -> 123 us (1.33)
  the two profiles are of different devices: /device:TPU:16 before, /device:TPU:14 now
where the time goes in v2:
time: 123 us; the launch traced here: 122 us
  Pallas kernels  122 us (99%)
    pallas_call x1, Pallas kernels, per_device(): pl.pallas_call(kernel, out_shape=shapes, in_specs=[hbm, hbm, hbm, vm, vm,...  68.7 us
    pallas_call x1, Pallas kernels, per_device(): pl.pallas_call(copy_kernel, out_shape=shapes, in_specs=[hbm] * len(shapes...  53 us

profile of v2, /device:TPU:14, one launch (start us, length us, event | category | flops | bytes accessed | tf_op | source)
XLA Modules:
  0.0 122.3 jit_solution(18331412097898660300)
XLA Ops:
  0.6 68.7 %shard_map.160 = (f32[2,256,256]{2,1,0:T(8,128)}, f32[2,256,256]{2,1,0:T(8,128)}, f32[2,256]{1,0:T(2,128)}, f32[2,256]{1,0:T(2,128)}, f32[256,256]{1,0:T(8,128)}...) custom-call(bf16[256,4096]{1,0:T(8,128)(2,1)} %tok.1, ...), custom_call_target="tpu_custom_call" | custom-call | flops 1073741824 | bytes 5242880 | tf_op jit(solution)/shard_map/pallas_call | solution.py:437
  69.3 53.0 %shard_map.161 = (f32[2,256,256]{2,1,0:T(8,128)}, f32[2,256,256]{2,1,0:T(8,128)}, f32[2,256]{1,0:T(2,128)}, f32[2,256]{1,0:T(2,128)}, f32[256,256]{1,0:T(8,128)}...) custom-call(f32[2,256,256]{2,1,0:T(8,128)} %get-tuple-element.27.refs_0_, ...), custom_call_target="tpu_custom_call" | custom-call | tf_op jit(solution)/shard_map/pallas_call | solution.py:474

commit v3 on v2

--- a/solution.py
+++ b/solution.py
@@ -41,9 +41,9 @@
 def kernel(
     tok, iw, ig, irow, icol, ow, og, orow, ocol,
     inew, iupd, irow_new, icol_new, onew, oupd, orow_new, ocol_new, hid,
-    g_v, w_v, raw, new_v, upd_v, tokbuf, agbuf, acc, zbuf, zout_v, zin_v, hid_v,
+    g_v, w_v, raw, tokbuf, agbuf, acc, zbuf, zout_v, zin_v,
     dp1, rx, rz, tx, tz, dp2, snd, scal, rmat,
-    load_sem, tok_sem, out_sem, st_send, st_recv, tx_send, tx_recv, sib_send, sib_recv,
+    load_sem, tok_sem, st_send, st_recv, tx_send, tx_recv, sib_send, sib_recv,
     ag_send, ag_recv, z_send, z_recv,
 ):
     dp, mp = lax.axis_index("dp"), lax.axis_index("mp")
@@ -59,10 +59,6 @@
     z_pair = (y * 2 + 1 - z, mp)
     sibling = (dp, mp + 1 - 2 * core)
 
-    barrier = pltpu.get_barrier_semaphore()
-    for peer in dp_peers + x_peers + zc_peers:
-        pl.semaphore_signal(barrier, inc=1, device_id=peer, device_id_type=MESH)
-
     loads = [
         pltpu.make_async_copy(ig, g_v.at[pl.ds(0, 2)], load_sem.at[0]),
         pltpu.make_async_copy(og, g_v.at[2], load_sem.at[1]),
@@ -71,15 +67,10 @@
     ]
     for c in loads:
         c.start()
-    own_tok = []
-    for b in range(NY):
-        c = pltpu.make_async_copy(
-            tok.at[:, pl.ds(pl.multiple_of((2 * b + z) * B, B), B)],
-            tokbuf.at[b, pl.ds(0, B), :],
-            tok_sem.at[b],
-        )
-        c.start()
-        own_tok.append(c)
+
+    barrier = pltpu.get_barrier_semaphore()
+    for peer in dp_peers + x_peers + zc_peers:
+        pl.semaphore_signal(barrier, inc=1, device_id=peer, device_id_type=MESH)
 
     def put(i, row, v):
         snd[i, row : row + 1, :] = v[:, :H]
@@ -164,8 +155,16 @@
     loads[2].wait()
     for c in range(EARLY):
         launch(c, w_v, c)
-    for c in range(EARLY):
-        launch(EARLY + c, g_v, c)
+    launch(EARLY, g_v, 0)
+    own_tok = []
+    for b in range(NY):
+        c = pltpu.make_async_copy(
+            tok.at[:, pl.ds(pl.multiple_of((2 * b + z) * B, B), B)],
+            tokbuf.at[b, pl.ds(0, B), :],
+            tok_sem.at[b],
+        )
+        c.start()
+        own_tok.append(c)
 
     tok_out = []
     for j in range(4):
@@ -194,6 +193,7 @@
         misc = jnp.where(lane1 == k, jnp.sum(v, axis=1, keepdims=True), misc)
 
     scal[0:8, :] = arrived(dp1, 0)
+    relay(0, 1)
     old = [icol[0:1, :], icol[1:2, :], orow[...]]
     fc = [FORGET * old[k] + FRESH * (take(2 * k) / D) for k in range(3)]
     cc = [lax.rsqrt(f) for f in fc]
@@ -212,27 +212,18 @@
     icol_new[1:2, :] = fc[1]
     orow_new[...] = fc[2]
 
+    relay(1, 1)
+    launch(EARLY + 1, g_v, 1)
     snd[3] = arrived(rx, 1)
     exchange(rz, zc, zc_peers, snd.at[3], 3)
-    for st in range(2 * EARLY):
-        relay(st, 1)
+    relay(2, 1)
+    relay(0, 2)
+    relay(1, 2)
     snd[4] = arrived(tx, 2)
     exchange(tz, zc, zc_peers, snd.at[4], 4)
-
-    sib_out = []
-    for j in range(4):
-        b = core * 4 + j
-        tok_out[j].wait_recv()
-        c = pltpu.make_async_remote_copy(
-            src_ref=tokbuf.at[b, pl.ds(B, B), :],
-            dst_ref=tokbuf.at[b, pl.ds(B, B), :],
-            send_sem=sib_send.at[j], recv_sem=sib_recv.at[j],
-            device_id=sibling, device_id_type=MESH,
-        )
-        c.start()
-        sib_out.append(c)
-    for st in range(2 * EARLY):
-        relay(st, 2)
+    relay(3, 1)
+    relay(0, 3)
+    relay(1, 3)
 
     scal[8:16, :] = arrived(rz, 3)
     scal[16:24, :] = arrived(tz, 4)
@@ -257,18 +248,31 @@
         raw[k] = raw[k] * jnp.concatenate([rr, rr], axis=1)
     raw[2] = raw[2] * lax.rsqrt(fr[2])
 
+    relay(2, 2)
+
+    sib_out = []
+    for j in range(4):
+        b = core * 4 + j
+        tok_out[j].wait_recv()
+        c = pltpu.make_async_remote_copy(
+            src_ref=tokbuf.at[b, pl.ds(B, B), :],
+            dst_ref=tokbuf.at[b, pl.ds(B, B), :],
+            send_sem=sib_send.at[j], recv_sem=sib_recv.at[j],
+            device_id=sibling, device_id_type=MESH,
+        )
+        c.start()
+        sib_out.append(c)
+    relay(3, 2)
+
     for c in own_tok:
         c.wait()
     for c in sib_out:
         c.wait()
     for st in range(EARLY):
         product(st, y, True)
-    for st in range(EARLY):
-        products(st, 1)
-    for st in range(2 * EARLY):
-        relay(st, 3)
-    for st in range(EARLY):
-        products(st, 2)
+        for t in range(1, 4):
+            products(st, t)
+    relay(2, 3)
 
     scal[0:8, :] = arrived(dp2, 5)
     s = [jnp.sum(scal[k : k + 1, :], axis=1, keepdims=True) for k in range(3)]
@@ -279,15 +283,27 @@
         step = RELATIVE * jnp.sqrt(scal[3:4, k : k + 1] / (D * FF))
         coef.append(step / clip * jnp.sqrt(mean[k]))
 
-    for k in range(2):
-        u = raw[k] * (-coef[k])
-        upd_v[k] = u
-        new_v[k] = w_v[k] + u
-    for c in range(EARLY, CHUNKS):
-        launch(EARLY + c, new_v, c)
-
-    for st in range(EARLY):
-        products(st, 3)
+    late = range(2 * EARLY, STREAMS)
+    for cols in (pl.ds(EARLY * C64, B - EARLY * C64), pl.ds(0, EARLY * C64)):
+        for k in range(2):
+            u = raw[k, :, cols] * (-coef[k])
+            iupd[k, :, cols] = u
+            inew[k, :, cols] = w_v[k, :, cols] + u
+        if cols.start:
+            for st in late:
+                launch(st, inew, st - EARLY)
+
+    def z_exchange(st):
+        i = st - EARLY
+        zout_v[i] = acc[st, B : 2 * B, :].astype(jnp.bfloat16)
+        c = pltpu.make_async_remote_copy(
+            src_ref=zout_v.at[i], dst_ref=zin_v.at[i],
+            send_sem=z_send.at[st], recv_sem=z_recv.at[st], device_id=z_pair, device_id_type=MESH,
+        )
+        c.start()
+        z_copies.append(c)
+
+    relay(3, 3)
     z_copies = []
     for st in range(EARLY):
         relay(st, 4)
@@ -298,32 +314,9 @@
         )
         c.start()
         z_copies.append(c)
-
-    def z_exchange(st):
-        i = st - EARLY
-        zout_v[i] = acc[st, B : 2 * B, :].astype(jnp.bfloat16)
-        c = pltpu.make_async_remote_copy(
-            src_ref=zout_v.at[i], dst_ref=zin_v.at[i],
-            send_sem=z_send.at[st], recv_sem=z_recv.at[st], device_id=z_pair, device_id_type=MESH,
-        )
-        c.start()
-        z_copies.append(c)
-
     u = raw[2] * (-coef[2])
-    upd_v[2] = u
-    new_v[2] = w_v[2] + u
-    outs = [
-        pltpu.make_async_copy(new_v.at[pl.ds(0, 2)], inew, out_sem.at[0]),
-        pltpu.make_async_copy(upd_v.at[pl.ds(0, 2)], iupd, out_sem.at[1]),
-        pltpu.make_async_copy(new_v.at[2], onew, out_sem.at[2]),
-        pltpu.make_async_copy(upd_v.at[2], oupd, out_sem.at[3]),
-    ]
-    for c in outs:
-        c.start()
-
-    late = range(2 * EARLY, STREAMS)
-    for st in late:
-        relay(st, 1)
+    oupd[...] = u
+    onew[...] = w_v[2] + u
 
     rmat[...] = jnp.ones((H, H), jnp.float32)
     for b in range(NY):
@@ -353,23 +346,25 @@
             else:
                 acc[st] += part
 
-    for b in range(0, 4):
+    for b in range(0, 3):
         scaled_products(b)
     for st in late:
-        product(st, y, True)
+        relay(st, 1)
+    for b in range(3, 6):
+        scaled_products(b)
     for st in late:
         relay(st, 2)
-    for b in range(4, NY):
+    for b in range(6, NY):
         scaled_products(b)
     for st in range(EARLY, 2 * EARLY):
         z_exchange(st)
     for st in late:
+        product(st, y, True)
         products(st, 1)
     for st in late:
         relay(st, 3)
     for st in late:
         products(st, 2)
-    for st in late:
         products(st, 3)
     for st in late:
         relay(st, 4)
@@ -377,15 +372,11 @@
         z_exchange(st)
 
     lane = lax.broadcasted_iota(jnp.int32, (B, H), 1)
-    hid_out = []
 
     def finish(p, left, right):
         gate = jnp.where(lane < C64, left, pltpu.roll(right, C64, 1))
         up = jnp.where(lane < C64, pltpu.roll(left, C64, 1), right)
-        hid_v[p] = (jax.nn.gelu(gate, approximate=True) * up).astype(jnp.bfloat16)
-        c = pltpu.make_async_copy(hid_v.at[p], hid.at[:, pl.ds(p * H, H)], out_sem.at[4 + p])
-        c.start()
-        hid_out.append(c)
+        hid[:, p * H : (p + 1) * H] = (jax.nn.gelu(gate, approximate=True) * up).astype(jnp.bfloat16)
 
     both = []
     for st in range(EARLY):
@@ -410,8 +401,6 @@
         for way in range(2):
             for t in range(1, steps(way, st) + 1):
                 ag_copy(way, st, t).wait_send()
-    for c in outs + hid_out:
-        c.wait()
 
 
 def copy_kernel(*refs):
@@ -436,12 +425,10 @@
     dma = pltpu.SemaphoreType.DMA
     outs = pl.pallas_call(
         kernel,
-        out_shape=shapes,
+        out_shape=tuple(pltpu.VMEM(a.shape, a.dtype) for a in shapes),
         in_specs=[hbm, hbm, hbm, vm, vm, hbm, hbm, vm, vm],
-        out_specs=(hbm, hbm, vm, vm, hbm, hbm, vm, vm, hbm),
+        out_specs=(vm,) * len(shapes),
         scratch_shapes=[
-            pltpu.VMEM((3, B, B), f32),
-            pltpu.VMEM((3, B, B), f32),
             pltpu.VMEM((3, B, B), f32),
             pltpu.VMEM((3, B, B), f32),
             pltpu.VMEM((3, B, B), f32),
@@ -451,7 +438,6 @@
             pltpu.VMEM((EARLY, B, H), f32),
             pltpu.VMEM((CHUNKS, B, H), bf16),
             pltpu.VMEM((CHUNKS, B, H), bf16),
-            pltpu.VMEM((CHUNKS // 2, B, H), bf16),
             pltpu.VMEM((16, 8, H), f32),
             pltpu.VMEM((8, 8, H), f32),
             pltpu.VMEM((8, 8, H), f32),
@@ -461,11 +447,11 @@
             pltpu.VMEM((6, 8, H), f32),
             pltpu.VMEM((24, H), f32),
             pltpu.VMEM((H, H), f32),
-            dma((4,)), dma((NY,)), dma((6,)), dma((6,)), dma((6,)), dma((4,)), dma((4,)), dma((4,)), dma((4,)),
+            dma((4,)), dma((NY,)), dma((6,)), dma((6,)), dma((4,)), dma((4,)), dma((4,)), dma((4,)),
             dma((2, STREAMS, 4)), dma((2, STREAMS, 4)), dma((STREAMS,)), dma((STREAMS,)),
         ],
         compiler_params=pltpu.CompilerParams(
-            collective_id=0, has_side_effects=True, vmem_limit_bytes=63 * 1024 * 1024
+            collective_id=0, has_side_effects=True, vmem_limit_bytes=61 * 1024 * 1024
         ),
         cost_estimate=pl.CostEstimate(
             flops=2 * B * D * 2 * B, bytes_accessed=5 * 1024 * 1024, transcendentals=B * B
@@ -474,10 +460,10 @@
     outs = pl.pallas_call(
         copy_kernel,
         out_shape=shapes,
-        in_specs=[hbm] * len(shapes),
+        in_specs=[vm] * len(shapes),
         out_specs=(hbm,) * len(shapes),
         scratch_shapes=[dma((len(shapes),))],
-    )(*outs)
+    )(*[pltpu.with_memory_space_constraint(o, pltpu.VMEM) for o in outs])
     outs = list(outs)
     outs[6] = outs[6].reshape(B)
     outs[7] = outs[7].reshape(B)

time: 123 us -> 69.6 us (0.57)
  Pallas kernels: 122 us -> 68.6 us
    pallas_call x2, Pallas kernels: 122 us -> 68.6 us  [the longest x1 67.4 us: per_device(): pl.pallas_call(kernel, out_shape=tuple((pltpu.VMEM(a.shape, a.dtype) for...]
where the time goes in v3:
time: 69.6 us; the launch traced here: 69.3 us
  Pallas kernels  68.6 us (99%)
    pallas_call x1, Pallas kernels, per_device(): pl.pallas_call(kernel, out_shape=tuple((pltpu.VMEM(a.shape, a.dtype) for...  67.4 us

profile of v3, /device:TPU:14, one launch (start us, length us, event | category | flops | bytes accessed | tf_op | source)
XLA Modules:
  0.0 69.3 jit_solution(14205214897401418700)
XLA Ops:
  0.6 67.4 %shard_map.160 = (f32[2,256,256]{2,1,0:T(8,128)S(1)}, f32[2,256,256]{2,1,0:T(8,128)S(1)}, f32[2,256]{1,0:T(2,128)S(1)}, f32[2,256]{1,0:T(2,128)S(1)}, f32[256,25...) custom-call(bf16[256,4096]{1,0:T(8,128)(2,1)} %tok.1, ...), custom_call_target="tpu_custom_call" | custom-call | flops 1073741824 | bytes 5242880 | tf_op jit(solution)/shard_map/pallas_call | solution.py:426
  68.0 1.3 %shard_map.161 = (f32[2,256,256]{2,1,0:T(8,128)}, f32[2,256,256]{2,1,0:T(8,128)}, f32[2,256]{1,0:T(2,128)}, f32[2,256]{1,0:T(2,128)}, f32[256,256]{1,0:T(8,128)}...) custom-call(f32[2,256,256]{2,1,0:T(8,128)S(1)} %get-tuple-element.27.refs_0_, ...), custom_call_target="tpu_custom_call" | custom-call | tf_op jit(solution)/shard_map/pallas_call | solution.py:460

commit v4 on v3

--- a/solution.py
+++ b/solution.py
@@ -41,10 +41,10 @@
 def kernel(
     tok, iw, ig, irow, icol, ow, og, orow, ocol,
     inew, iupd, irow_new, icol_new, onew, oupd, orow_new, ocol_new, hid,
-    g_v, w_v, raw, tokbuf, agbuf, acc, zbuf, zout_v, zin_v,
+    g_v, w_v, raw, late_w, late_raw, tokbuf, tok_far, xbuf, agbuf, acc, zbuf, zout_v, zin_v,
     dp1, rx, rz, tx, tz, dp2, snd, scal, rmat,
     load_sem, tok_sem, st_send, st_recv, tx_send, tx_recv, sib_send, sib_recv,
-    ag_send, ag_recv, z_send, z_recv,
+    ag_send, ag_recv, x_send, x_recv, z_send, z_recv,
 ):
     dp, mp = lax.axis_index("dp"), lax.axis_index("mp")
     y, z = dp // 2, lax.rem(dp, 2)
@@ -57,6 +57,9 @@
     y_next = (lax.rem(y + 1, NY) * 2 + z, mp)
     y_prev = (lax.rem(y + NY - 1, NY) * 2 + z, mp)
     z_pair = (y * 2 + 1 - z, mp)
+    y_next_pair = (lax.rem(y + 1, NY) * 2 + 1 - z, mp)
+    y_prev_pair = (lax.rem(y + NY - 1, NY) * 2 + 1 - z, mp)
+    across = lax.rem(y + 4, NY)
     sibling = (dp, mp + 1 - 2 * core)
 
     loads = [
@@ -100,13 +103,18 @@
         part = slot.at[pl.ds(0, slot.shape[0] - 1)]
         pltpu.make_async_copy(part, part, st_send.at[stage]).wait()
 
-    def ag_copy(way, st, s):
+    def ag_copy(way, st, s, h):
         src = lax.rem(y + NY - (s - 1), NY) if way == 0 else lax.rem(y + s - 1, NY)
+        rows = B // pieces(st)
+        part = agbuf.at[st, src, pl.ds(h * rows, rows), :]
         return pltpu.make_async_remote_copy(
-            src_ref=agbuf.at[st, src], dst_ref=agbuf.at[st, src],
-            send_sem=ag_send.at[way, st, s - 1], recv_sem=ag_recv.at[way, st, s - 1],
+            src_ref=part, dst_ref=part,
+            send_sem=ag_send.at[way, st, s - 1, h], recv_sem=ag_recv.at[way, st, s - 1, h],
             device_id=y_next if way == 0 else y_prev, device_id_type=MESH,
         )
+
+    def pieces(st):
+        return 1 if st < 2 * EARLY else 2
 
     def steps(way, st):
         return 4 if (st % 2 == 0) == (way == 0) else 3
@@ -114,19 +122,38 @@
     def origin(way, s):
         return lax.rem(y + NY - s, NY) if way == 0 else lax.rem(y + s, NY)
 
-    def launch(st, pair, c):
+    def pack(pair, c):
         lo = c * C64
-        block = jnp.concatenate([pair[0, :, lo : lo + C64], pair[1, :, lo : lo + C64]], axis=1)
+        return jnp.concatenate([pair[0, :, lo : lo + C64], pair[1, :, lo : lo + C64]], axis=1)
+
+    def launch(st, block):
         agbuf[st, y] = block.astype(jnp.bfloat16)
-        for way in range(2):
-            ag_copy(way, st, 1).start()
+        for h in range(pieces(st)):
+            for way in range(2):
+                ag_copy(way, st, 1, h).start()
+
+    def far_copy(way, st, h):
+        rows = B // pieces(st)
+        src = lax.rem(y + NY - 3, NY) if way == 0 else lax.rem(y + 3, NY)
+        return pltpu.make_async_remote_copy(
+            src_ref=agbuf.at[st, src, pl.ds(h * rows, rows), :],
+            dst_ref=xbuf.at[st - 2 * EARLY, pl.ds(h * rows, rows), :],
+            send_sem=x_send.at[st - 2 * EARLY, h], recv_sem=x_recv.at[st - 2 * EARLY, h],
+            device_id=y_next_pair if way == 0 else y_prev_pair, device_id_type=MESH,
+        )
+
+    def far_way(st):
+        return 0 if steps(0, st) == 4 else 1
 
     def relay(st, s):
-        for way in range(2):
-            if s <= steps(way, st):
-                ag_copy(way, st, s).wait_recv()
-                if s < steps(way, st):
-                    ag_copy(way, st, s + 1).start()
+        for h in range(pieces(st)):
+            for way in range(2):
+                if s <= steps(way, st):
+                    ag_copy(way, st, s, h).wait_recv()
+                    if s < steps(way, st):
+                        ag_copy(way, st, s + 1, h).start()
+                        if s == 3 and st >= 2 * EARLY:
+                            far_copy(way, st, h).start()
 
     def product(st, b, first=False):
         part = jnp.dot(tokbuf[b], agbuf[st, b], preferred_element_type=jnp.float32)
@@ -154,9 +181,15 @@
 
     loads[2].wait()
     for c in range(EARLY):
-        launch(c, w_v, c)
-    launch(EARLY, g_v, 0)
-    own_tok = []
+        launch(c, pack(w_v, c))
+    for c in range(EARLY):
+        launch(EARLY + c, pack(g_v, c))
+    own_tok = [
+        pltpu.make_async_copy(
+            tok.at[:, pl.ds(pl.multiple_of((2 * across + 1 - z) * B, B), B)], tok_far, tok_sem.at[NY]
+        )
+    ]
+    own_tok[0].start()
     for b in range(NY):
         c = pltpu.make_async_copy(
             tok.at[:, pl.ds(pl.multiple_of((2 * b + z) * B, B), B)],
@@ -213,17 +246,17 @@
     orow_new[...] = fc[2]
 
     relay(1, 1)
-    launch(EARLY + 1, g_v, 1)
     snd[3] = arrived(rx, 1)
     exchange(rz, zc, zc_peers, snd.at[3], 3)
     relay(2, 1)
+    relay(3, 1)
     relay(0, 2)
-    relay(1, 2)
     snd[4] = arrived(tx, 2)
     exchange(tz, zc, zc_peers, snd.at[4], 4)
-    relay(3, 1)
+    relay(1, 2)
+    relay(2, 2)
+    relay(3, 2)
     relay(0, 3)
-    relay(1, 3)
 
     scal[8:16, :] = arrived(rz, 3)
     scal[16:24, :] = arrived(tz, 4)
@@ -247,8 +280,7 @@
         rr = lanes_to_rows(lax.rsqrt(fr[k]))
         raw[k] = raw[k] * jnp.concatenate([rr, rr], axis=1)
     raw[2] = raw[2] * lax.rsqrt(fr[2])
-
-    relay(2, 2)
+    relay(1, 3)
 
     sib_out = []
     for j in range(4):
@@ -262,7 +294,12 @@
         )
         c.start()
         sib_out.append(c)
-    relay(3, 2)
+    relay(2, 3)
+    late = range(2 * EARLY, STREAMS)
+    for st in late:
+        late_w[st - 2 * EARLY] = pack(w_v, st - EARLY)
+        late_raw[st - 2 * EARLY] = pack(raw, st - EARLY)
+    relay(3, 3)
 
     for c in own_tok:
         c.wait()
@@ -272,7 +309,6 @@
         product(st, y, True)
         for t in range(1, 4):
             products(st, t)
-    relay(2, 3)
 
     scal[0:8, :] = arrived(dp2, 5)
     s = [jnp.sum(scal[k : k + 1, :], axis=1, keepdims=True) for k in range(3)]
@@ -283,15 +319,14 @@
         step = RELATIVE * jnp.sqrt(scal[3:4, k : k + 1] / (D * FF))
         coef.append(step / clip * jnp.sqrt(mean[k]))
 
-    late = range(2 * EARLY, STREAMS)
-    for cols in (pl.ds(EARLY * C64, B - EARLY * C64), pl.ds(0, EARLY * C64)):
-        for k in range(2):
-            u = raw[k, :, cols] * (-coef[k])
-            iupd[k, :, cols] = u
-            inew[k, :, cols] = w_v[k, :, cols] + u
-        if cols.start:
-            for st in late:
-                launch(st, inew, st - EARLY)
+    both_coef = jnp.where(lane1 < C64, coef[0], coef[1])
+    for st in late:
+        i = st - 2 * EARLY
+        launch(st, late_w[i] + late_raw[i] * (-both_coef))
+    for k in range(2):
+        u = raw[k] * (-coef[k])
+        iupd[k] = u
+        inew[k] = w_v[k] + u
 
     def z_exchange(st):
         i = st - EARLY
@@ -303,7 +338,6 @@
         c.start()
         z_copies.append(c)
 
-    relay(3, 3)
     z_copies = []
     for st in range(EARLY):
         relay(st, 4)
@@ -361,14 +395,11 @@
     for st in late:
         product(st, y, True)
         products(st, 1)
+        products(st, 2)
     for st in late:
         relay(st, 3)
     for st in late:
-        products(st, 2)
         products(st, 3)
-    for st in late:
-        relay(st, 4)
-        products(st, 4)
         z_exchange(st)
 
     lane = lax.broadcasted_iota(jnp.int32, (B, H), 1)
@@ -387,20 +418,37 @@
         step_part = acc[EARLY + st, 0:B, :] + zin_v[st].astype(jnp.float32)
         both.append(acc[st, 0:B, :] + zbuf[st] - step_part * scale)
     finish(0, both[0], both[1])
-    both = []
-    for st in late:
-        z_copies[st].wait_recv()
-        both.append(acc[st, 0:B, :] + zin_v[st - EARLY].astype(jnp.float32))
-    finish(1, both[0], both[1])
-
     for stage, slot in enumerate((dp1, rx, tx, rz, tz, dp2)):
         sent(slot, stage)
-    for c in tok_out + z_copies:
+    for c in tok_out + z_copies[: 2 * EARLY]:
         c.wait_send()
-    for st in range(STREAMS):
+
+    def left(st):
         for way in range(2):
             for t in range(1, steps(way, st) + 1):
-                ag_copy(way, st, t).wait_send()
+                for h in range(pieces(st)):
+                    ag_copy(way, st, t, h).wait_send()
+
+    for st in range(2 * EARLY):
+        left(st)
+
+    both = []
+    for st in late:
+        relay(st, 4)
+        i = st - 2 * EARLY
+        part = jnp.dot(tokbuf[across, 0:B, :], agbuf[st, across], preferred_element_type=jnp.float32)
+        z_copies[st].wait_recv()
+        part += acc[st, 0:B, :] + zin_v[st - EARLY].astype(jnp.float32)
+        for h in range(pieces(st)):
+            far_copy(far_way(st), st, h).wait_recv()
+        both.append(part + jnp.dot(tok_far[...], xbuf[i], preferred_element_type=jnp.float32))
+    finish(1, both[0], both[1])
+
+    for st in late:
+        left(st)
+        z_copies[st].wait_send()
+        for h in range(pieces(st)):
+            far_copy(far_way(st), st, h).wait_send()
 
 
 def copy_kernel(*refs):
@@ -432,7 +480,11 @@
             pltpu.VMEM((3, B, B), f32),
             pltpu.VMEM((3, B, B), f32),
             pltpu.VMEM((3, B, B), f32),
+            pltpu.VMEM((CHUNKS - EARLY, B, H), f32),
+            pltpu.VMEM((CHUNKS - EARLY, B, H), f32),
             pltpu.VMEM((NY, 2 * B, B), bf16),
+            pltpu.VMEM((B, B), bf16),
+            pltpu.VMEM((CHUNKS - EARLY, B, H), bf16),
             pltpu.VMEM((STREAMS, NY, B, H), bf16),
             pltpu.VMEM((STREAMS, 2 * B, H), f32),
             pltpu.VMEM((EARLY, B, H), f32),
@@ -447,8 +499,8 @@
             pltpu.VMEM((6, 8, H), f32),
             pltpu.VMEM((24, H), f32),
             pltpu.VMEM((H, H), f32),
-            dma((4,)), dma((NY,)), dma((6,)), dma((6,)), dma((4,)), dma((4,)), dma((4,)), dma((4,)),
-            dma((2, STREAMS, 4)), dma((2, STREAMS, 4)), dma((STREAMS,)), dma((STREAMS,)),
+            dma((4,)), dma((NY + 1,)), dma((6,)), dma((6,)), dma((4,)), dma((4,)), dma((4,)), dma((4,)),
+            dma((2, STREAMS, 4, 2)), dma((2, STREAMS, 4, 2)), dma((CHUNKS - EARLY, 2)), dma((CHUNKS - EARLY, 2)), dma((STREAMS,)), dma((STREAMS,)),
         ],
         compiler_params=pltpu.CompilerParams(
             collective_id=0, has_side_effects=True, vmem_limit_bytes=61 * 1024 * 1024

time: 69.6 us -> 68.1 us (0.978)
  Pallas kernels: 68.6 us -> 67.2 us
    pallas_call x1, Pallas kernels: 67.4 us -> 65.9 us  [per_device(): pl.pallas_call(kernel, out_shape=tuple((pltpu.VMEM(a.shape, a.dtype) for...]
where the time goes in v4:
time: 68.1 us; the launch traced here: 67.8 us
  Pallas kernels  67.2 us (99%)
    pallas_call x1, Pallas kernels, per_device(): pl.pallas_call(kernel, out_shape=tuple((pltpu.VMEM(a.shape, a.dtype) for...  65.9 us

profile of v4, /device:TPU:14, one launch (start us, length us, event | category | flops | bytes accessed | tf_op | source)
XLA Modules:
  0.0 67.8 jit_solution(15319553012343797188)
XLA Ops:
  0.6 65.9 %shard_map.160 = (f32[2,256,256]{2,1,0:T(8,128)S(1)}, f32[2,256,256]{2,1,0:T(8,128)S(1)}, f32[2,256]{1,0:T(2,128)S(1)}, f32[2,256]{1,0:T(2,128)S(1)}, f32[256,25...) custom-call(bf16[256,4096]{1,0:T(8,128)(2,1)} %tok.1, ...), custom_call_target="tpu_custom_call" | custom-call | flops 1073741824 | bytes 5242880 | tf_op jit(solution)/shard_map/pallas_call | solution.py:474
  66.6 1.3 %shard_map.161 = (f32[2,256,256]{2,1,0:T(8,128)}, f32[2,256,256]{2,1,0:T(8,128)}, f32[2,256]{1,0:T(2,128)}, f32[2,256]{1,0:T(2,128)}, f32[256,256]{1,0:T(8,128)}...) custom-call(f32[2,256,256]{2,1,0:T(8,128)S(1)} %get-tuple-element.27.refs_0_, ...), custom_call_target="tpu_custom_call" | custom-call | tf_op jit(solution)/shard_map/pallas_call | solution.py:512

commit v5 on v4

--- a/solution.py
+++ b/solution.py
@@ -226,7 +226,6 @@
         misc = jnp.where(lane1 == k, jnp.sum(v, axis=1, keepdims=True), misc)
 
     scal[0:8, :] = arrived(dp1, 0)
-    relay(0, 1)
     old = [icol[0:1, :], icol[1:2, :], orow[...]]
     fc = [FORGET * old[k] + FRESH * (take(2 * k) / D) for k in range(3)]
     cc = [lax.rsqrt(f) for f in fc]
@@ -245,18 +244,49 @@
     icol_new[1:2, :] = fc[1]
     orow_new[...] = fc[2]
 
+    relay(0, 1)
     relay(1, 1)
     snd[3] = arrived(rx, 1)
     exchange(rz, zc, zc_peers, snd.at[3], 3)
     relay(2, 1)
     relay(3, 1)
-    relay(0, 2)
     snd[4] = arrived(tx, 2)
     exchange(tz, zc, zc_peers, snd.at[4], 4)
-    relay(1, 2)
-    relay(2, 2)
-    relay(3, 2)
-    relay(0, 3)
+    for st in range(2 * EARLY):
+        relay(st, 2)
+    sib_out = []
+    for j in range(4):
+        b = core * 4 + j
+        tok_out[j].wait_recv()
+        c = pltpu.make_async_remote_copy(
+            src_ref=tokbuf.at[b, pl.ds(B, B), :],
+            dst_ref=tokbuf.at[b, pl.ds(B, B), :],
+            send_sem=sib_send.at[j], recv_sem=sib_recv.at[j],
+            device_id=sibling, device_id_type=MESH,
+        )
+        c.start()
+        sib_out.append(c)
+    for t in (3, 4):
+        for st in range(2 * EARLY):
+            relay(st, t)
+
+    for c in own_tok:
+        c.wait()
+    for c in sib_out:
+        c.wait()
+    for st in range(EARLY):
+        product(st, y, True)
+        for t in range(1, 4):
+            products(st, t)
+    z_copies = []
+    for st in range(EARLY):
+        products(st, 4)
+        c = pltpu.make_async_remote_copy(
+            src_ref=acc.at[st, pl.ds(B, B), :], dst_ref=zbuf.at[st],
+            send_sem=z_send.at[st], recv_sem=z_recv.at[st], device_id=z_pair, device_id_type=MESH,
+        )
+        c.start()
+        z_copies.append(c)
 
     scal[8:16, :] = arrived(rz, 3)
     scal[16:24, :] = arrived(tz, 4)
@@ -280,36 +310,11 @@
         rr = lanes_to_rows(lax.rsqrt(fr[k]))
         raw[k] = raw[k] * jnp.concatenate([rr, rr], axis=1)
     raw[2] = raw[2] * lax.rsqrt(fr[2])
-    relay(1, 3)
-
-    sib_out = []
-    for j in range(4):
-        b = core * 4 + j
-        tok_out[j].wait_recv()
-        c = pltpu.make_async_remote_copy(
-            src_ref=tokbuf.at[b, pl.ds(B, B), :],
-            dst_ref=tokbuf.at[b, pl.ds(B, B), :],
-            send_sem=sib_send.at[j], recv_sem=sib_recv.at[j],
-            device_id=sibling, device_id_type=MESH,
-        )
-        c.start()
-        sib_out.append(c)
-    relay(2, 3)
+
     late = range(2 * EARLY, STREAMS)
     for st in late:
         late_w[st - 2 * EARLY] = pack(w_v, st - EARLY)
         late_raw[st - 2 * EARLY] = pack(raw, st - EARLY)
-    relay(3, 3)
-
-    for c in own_tok:
-        c.wait()
-    for c in sib_out:
-        c.wait()
-    for st in range(EARLY):
-        product(st, y, True)
-        for t in range(1, 4):
-            products(st, t)
-
     scal[0:8, :] = arrived(dp2, 5)
     s = [jnp.sum(scal[k : k + 1, :], axis=1, keepdims=True) for k in range(3)]
     mean = [jnp.sum(take(4 + 2 * k), axis=1, keepdims=True) / D for k in range(2)] + [mean2]
@@ -338,16 +343,6 @@
         c.start()
         z_copies.append(c)
 
-    z_copies = []
-    for st in range(EARLY):
-        relay(st, 4)
-        products(st, 4)
-        c = pltpu.make_async_remote_copy(
-            src_ref=acc.at[st, pl.ds(B, B), :], dst_ref=zbuf.at[st],
-            send_sem=z_send.at[st], recv_sem=z_recv.at[st], device_id=z_pair, device_id_type=MESH,
-        )
-        c.start()
-        z_copies.append(c)
     u = raw[2] * (-coef[2])
     oupd[...] = u
     onew[...] = w_v[2] + u
@@ -356,8 +351,6 @@
     for b in range(NY):
         rmat[4 * b : 4 * b + 4, :] = lax.rsqrt(dp2[2 * b + z, 4:8, :])
     rmat[...] = rmat[...].T
-    for st in range(EARLY, 2 * EARLY):
-        relay(st, 4)
     low = lax.broadcasted_iota(jnp.int32, (H, H), 1) < C64
 
     def scaled_products(b):

time: 68.1 us -> 74.1 us (1.088)
  Pallas kernels: 67.2 us -> 73.2 us
    pallas_call x1, Pallas kernels: 65.9 us -> 72 us  [per_device(): pl.pallas_call(kernel, out_shape=tuple((pltpu.VMEM(a.shape, a.dtype) for...]
where the time goes in v5:
time: 74.1 us; the launch traced here: 73.9 us
  Pallas kernels  73.2 us (99%)
    pallas_call x1, Pallas kernels, per_device(): pl.pallas_call(kernel, out_shape=tuple((pltpu.VMEM(a.shape, a.dtype) for...  72 us

profile of v5, /device:TPU:14, one launch (start us, length us, event | category | flops | bytes accessed | tf_op | source)
XLA Modules:
  0.0 73.9 jit_solution(10739948377459495247)
XLA Ops:
  0.6 72.0 %shard_map.160 = (f32[2,256,256]{2,1,0:T(8,128)S(1)}, f32[2,256,256]{2,1,0:T(8,128)S(1)}, f32[2,256]{1,0:T(2,128)S(1)}, f32[2,256]{1,0:T(2,128)S(1)}, f32[256,25...) custom-call(bf16[256,4096]{1,0:T(8,128)(2,1)} %tok.1, ...), custom_call_target="tpu_custom_call" | custom-call | flops 1073741824 | bytes 5242880 | tf_op jit(solution)/shard_map/pallas_call | solution.py:467
  72.6 1.3 %shard_map.161 = (f32[2,256,256]{2,1,0:T(8,128)}, f32[2,256,256]{2,1,0:T(8,128)}, f32[2,256]{1,0:T(2,128)}, f32[2,256]{1,0:T(2,128)}, f32[256,256]{1,0:T(8,128)}...) custom-call(f32[2,256,256]{2,1,0:T(8,128)S(1)} %get-tuple-element.27.refs_0_, ...), custom_call_target="tpu_custom_call" | custom-call | tf_op jit(solution)/shard_map/pallas_call | solution.py:505
